TPU v7x, 128 devices: a whole 4x4x4 slice. The times are simulated.
128 devices in a mesh: dp: 4 (over z_lo, core), fsdp: 32 (over z_hi, x, y).
Axes of the slice: x: 4, y: 4, z: 4 (z_hi: 2, z_lo: 2; z = z_hi * 2 + z_lo), core: 2. Of those that a mesh axis runs over, the one named last changes fastest.
Arguments:
- feat_s: bfloat16 [16384, 6144], P(('dp', 'fsdp')), may hold values from -6 to 6
- feat_t: bfloat16 [16384, 6144], P(('dp', 'fsdp')), may hold values from -6 to 6
- bot_s: float32 [6144, 256], P(('dp', 'fsdp')), may hold values from -0.078125 to 0.078125
- bot_m: float32 [6144, 256], P(('dp', 'fsdp')), may hold values from -0.006 to 0.006
- bot_v: float32 [6144, 256], P(('dp', 'fsdp')), may hold values from 1e-07 to 1e-05
- bot_t: float32 [6144, 256], P(('dp', 'fsdp')), may hold values from -0.078125 to 0.078125
- proto_s: float32 [256, 32768], P(None, ('fsdp', 'dp')), may hold values from -0.1 to 0.1
- proto_m: float32 [256, 32768], P(None, ('fsdp', 'dp')), may hold values from -0.006 to 0.006
- proto_v: float32 [256, 32768], P(None, ('fsdp', 'dp')), may hold values from 1e-07 to 1e-05
- proto_t: float32 [256, 32768], P(None, ('fsdp', 'dp')), may hold values from -0.1 to 0.1
Outputs:
- new_bot_s: float32 [6144, 256], P(('dp', 'fsdp'))
- new_bot_m: float32 [6144, 256], P(('dp', 'fsdp'))
- new_bot_v: float32 [6144, 256], P(('dp', 'fsdp'))
- new_bot_t: float32 [6144, 256], P(('dp', 'fsdp'))
- new_proto_s: float32 [256, 32768], P(None, ('fsdp', 'dp'))
- new_proto_m: float32 [256, 32768], P(None, ('fsdp', 'dp'))
- new_proto_v: float32 [256, 32768], P(None, ('fsdp', 'dp'))
- new_proto_t: float32 [256, 32768], P(None, ('fsdp', 'dp'))
All inputs are finite; a program needn't handle non-finite values.
Results may differ from a plain program's by a relative error of at most 0.0045.
The roundings to bfloat16 on the way count: a program that leaves them out, or rounds other values in their place, can miss the bound.
Values may be sent and summed in bfloat16 or wider, within the bound.
A program may use at most 128 MiB of HBM per device.

v0:
```python
import jax
import jax.numpy as jnp
from jax import lax
from jax.sharding import PartitionSpec as P

tau_student = 0.1
tau_teacher = 0.04
bias_first = 0.99997343860111
bias_second = 0.0952078527


def adamw(param, first, second, grad, teacher):
    first_new = 0.9 * first + 0.1 * grad
    second_new = 0.999 * second + 0.001 * grad * grad
    direction = first_new / bias_first / (jnp.sqrt(second_new / bias_second) + 1e-08)
    param_new = param - 0.002 * (direction + 0.04 * param)
    teacher_new = 0.996 * teacher + 0.004 * param_new
    return (param_new, first_new, second_new, teacher_new)


def per_device(feat_s, feat_t, bot_s, bot_m, bot_v, bot_t, proto_s, proto_m, proto_v, proto_t):
    cols_t = feat_t
    ys = jnp.dot(
        feat_s,
        lax.all_gather(bot_s.astype(jnp.bfloat16), ("dp", "fsdp"), axis=0, tiled=True),
        preferred_element_type=jnp.float32,
    )
    yt = jnp.dot(
        cols_t,
        lax.all_gather(bot_t.astype(jnp.bfloat16), ("dp", "fsdp"), axis=0, tiled=True),
        preferred_element_type=jnp.float32,
    )
    norm_s = jnp.sqrt(jnp.sum(ys * ys, axis=1, keepdims=True) + 1e-06)
    norm_t = jnp.sqrt(jnp.sum(yt * yt, axis=1, keepdims=True) + 1e-06)
    unit_s = ys / norm_s
    codes_s = unit_s.astype(jnp.bfloat16)
    codes_t = (yt / norm_t).astype(jnp.bfloat16)
    half_s = proto_s.astype(jnp.bfloat16)
    half_t = proto_t.astype(jnp.bfloat16)
    cols_s, cols_t = (
        lax.all_gather(half_s, "dp", axis=1, tiled=True),
        lax.all_gather(half_t, "dp", axis=1, tiled=True),
    )
    all_s, all_t = (
        lax.all_gather(codes_s, "fsdp", axis=0, tiled=True),
        lax.all_gather(codes_t, "fsdp", axis=0, tiled=True),
    )
    expo_s = jnp.exp(jnp.dot(all_s, cols_s, preferred_element_type=jnp.float32) / tau_student)
    expo_t = jnp.exp(jnp.dot(all_t, cols_t, preferred_element_type=jnp.float32) / tau_teacher)
    total_s, total_t = lax.psum((jnp.sum(expo_s, axis=1), jnp.sum(expo_t, axis=1)), "fsdp")
    dz = ((expo_s / total_s[:, None] - expo_t / total_t[:, None]) / tau_student).astype(
        jnp.bfloat16
    )
    part_proto = lax.dot_general(
        all_s, dz, (((0,), (0,)), ((), ())), preferred_element_type=jnp.float32
    )
    g_proto = lax.psum_scatter(part_proto, "dp", scatter_dimension=1, tiled=True)
    dh = lax.psum_scatter(
        lax.dot_general(dz, cols_s, (((1,), (1,)), ((), ())), preferred_element_type=jnp.float32),
        "fsdp",
        scatter_dimension=0,
        tiled=True,
    )
    dy = ((dh - unit_s * jnp.sum(unit_s * dh, axis=1, keepdims=True)) / norm_s).astype(jnp.bfloat16)
    g_bot = lax.psum_scatter(
        lax.dot_general(feat_s, dy, (((0,), (0,)), ((), ())), preferred_element_type=jnp.float32),
        ("dp", "fsdp"),
        scatter_dimension=0,
        tiled=True,
    )
    b_s, b_m, b_v, b_t = adamw(bot_s, bot_m, bot_v, g_bot, bot_t)
    p_s, p_m, p_v, p_t = adamw(proto_s, proto_m, proto_v, g_proto, proto_t)
    return (b_s, b_m, b_v, b_t, p_s, p_m, p_v, p_t)


def solution(mesh):
    return jax.shard_map(
        per_device,
        mesh=mesh,
        in_specs=(
            P(("dp", "fsdp"), None),
            P(("dp", "fsdp"), None),
            P(("dp", "fsdp"), None),
            P(("dp", "fsdp"), None),
            P(("dp", "fsdp"), None),
            P(("dp", "fsdp"), None),
            P(None, ("fsdp", "dp")),
            P(None, ("fsdp", "dp")),
            P(None, ("fsdp", "dp")),
            P(None, ("fsdp", "dp")),
        ),
        out_specs=(
            P(("dp", "fsdp"), None),
            P(("dp", "fsdp"), None),
            P(("dp", "fsdp"), None),
            P(("dp", "fsdp"), None),
            P(None, ("fsdp", "dp")),
            P(None, ("fsdp", "dp")),
            P(None, ("fsdp", "dp")),
            P(None, ("fsdp", "dp")),
        ),
        check_vma=False,
    )
```

profile of v0, /device:TPU:96, one launch (start us, length us, event | category | flops | bytes accessed | tf_op | source)
XLA Modules:
  0.0 1919.9 jit_solution(14475440207048507038)
XLA Ops:
  7.2 0.0 copy-start
  7.2 0.0 copy-start.2
  7.2 0.0 copy-start.3
  7.2 0.0 all-gather.9.cloned.1.call-start
  7.2 1.5 convert_element_type.27
  8.8 0.0 all-gather.9.cloned.1.call-update
  8.8 0.0 all-gather.5.cloned.1.call-start
  8.9 1.4 convert_element_type.24
  10.3 0.0 all-gather.5.cloned.1.call-update
  10.3 0.0 all-gather.11.cloned.1.call-start
  10.4 304.5 %all-gather.9.cloned.1.call-done = bf16[6144,256]{1,0:T(8,128)(2,1)} async-done(((bf16[48,256]{1,0:T(8,128)(2,1)}), bf16[6144,256]{1,0:T(8,128)(2,1)}) %all-gather.9.cloned.1.call-update) | async-done | bytes 3145744 | tf_op jit(solution)/shard_map/all_gather | solution.py:30
  314.8 3.0 multiply_reduce_fusion.1
  317.9 0.7 divide_convert_fusion.1
  318.6 0.0 all-gather.11.cloned.1.call-update
  318.6 0.0 all-gather.7.cloned.1.call-start
  318.7 304.1 %all-gather.5.cloned.1.call-done = bf16[6144,256]{1,0:T(8,128)(2,1)} async-done(((bf16[48,256]{1,0:T(8,128)(2,1)}), bf16[6144,256]{1,0:T(8,128)(2,1)}) %all-gather.5.cloned.1.call-update) | async-done | bytes 3145744 | tf_op jit(solution)/shard_map/all_gather | solution.py:25
  622.7 0.0 copy-done
  622.7 2.5 multiply_reduce_fusion.2
  625.3 0.7 fusion.6
  626.0 0.0 all-gather.7.cloned.1.call-update
  626.1 0.0 reduce-scatter.6.cloned.1.call-start
  626.1 0.0 copy-done.2
  626.1 0.0 copy-done.3
  626.2 7.8 all_gather.20
  633.9 7.3 all_gather.23
  641.2 58.3 %all-gather.11.cloned.1.call-done = bf16[4096,256]{1,0:T(8,128)(2,1)} async-done(((bf16[128,256]{1,0:T(8,128)(2,1)}), bf16[4096,256]{1,0:T(8,128)(2,1)}) %all-gather.11.cloned.1.call-update) | async-done | bytes 2097168 | tf_op jit(solution)/shard_map/all_gather | solution.py:46
  699.5 8.7 fusion.1
  708.2 64.0 %all-gather.7.cloned.1.call-done = bf16[4096,256]{1,0:T(8,128)(2,1)} async-done(((bf16[128,256]{1,0:T(8,128)(2,1)}), bf16[4096,256]{1,0:T(8,128)(2,1)}) %all-gather.7.cloned.1.call-update) | async-done | bytes 2097168 | tf_op jit(solution)/shard_map/all_gather | solution.py:45
  772.2 8.7 fusion
  780.9 180.6 %all-reduce = (f32[4096]{0:T(1024)S(1)}, f32[4096]{0:T(1024)S(1)}) all-reduce(f32[4096]{0:T(1024)S(1)} %get-tuple-element.38, f32[4096]{0:T(1024)S(1)} %get-tuple-element.40), channel_id=1, replica_groups=mesh['dp'=4,'fsdp'=32] {'fsdp'}, use_global_device_ids=true, to_apply=%region_5.0 | all-reduce | flops 8192 | bytes 65536 | tf_op jit(solution)/shard_map/psum | solution.py:50
  961.4 12.5 multiply_convert_fusion
  973.9 0.0 copy-start.1
  973.9 3.2 copy-done.1
  977.1 4.6 fusion.9
  981.7 0.0 reduce-scatter.6.cloned.1.call-update
  981.8 0.2 reduce-scatter.8.cloned.1.call-start
  982.0 7.5 fusion.10
  989.4 0.0 reduce-scatter.8.cloned.1.call-update
  989.5 0.0 reduce-scatter.10.cloned.1.call-start
  989.5 179.3 %reduce-scatter.6.cloned.1.call-done = f32[128,256]{1,0:T(8,128)} async-done(((f32[4096,256]{1,0:T(8,128)}), f32[128,256]{1,0:T(8,128)}) %reduce-scatter.6.cloned.1.call-update) | async-done | bytes 131088 | tf_op jit(solution)/shard_map/reduce_scatter | solution.py:58
  1168.9 1.1 multiply_reduce_fusion
  1169.9 4.7 convolution_bitcast_fusion
  1174.6 6.6 copy.39
  1181.2 0.0 copy-start.4
  1181.2 0.0 copy-start.5
  1181.2 0.0 copy-start.6
  1181.2 0.0 copy-start.7
  1181.2 0.0 copy-start.8
  1181.2 0.0 copy-start.9
  1181.2 0.0 reduce-scatter.10.cloned.1.call-update
  1181.2 6.0 reduce-scatter.8.cloned.1.call-done
  1187.3 0.0 copy-done.4
  1187.3 0.0 copy-done.5
  1187.3 2.1 multiply_add_fusion
  1189.3 722.2 %reduce-scatter.10.cloned.1.call-done = f32[48,256]{1,0:T(8,128)} async-done(((f32[6144,256]{1,0:T(8,128)}), f32[48,256]{1,0:T(8,128)}) %reduce-scatter.10.cloned.1.call-update) | async-done | bytes 49168 | tf_op jit(solution)/shard_map/reduce_scatter | solution.py:65
  1911.5 0.0 copy-done.6
  1911.5 0.0 copy-done.7
  1911.5 0.0 copy-done.8
  1911.5 0.0 copy-done.9
  1911.5 1.5 multiply_add_fusion.2
  (4 shorter events, 0.1 us)
Async XLA Ops:
  7.2 615.6 %copy-start = (bf16[128,6144]{1,0:T(8,128)(2,1)S(1)}, bf16[128,6144]{1,0:T(8,128)(2,1)}, u32[]{:S(2)}) copy-start(bf16[128,6144]{1,0:T(8,128)(2,1)} %param.10) | copy-start | bytes 4718596
  7.2 618.9 %copy-start.2 = (f32[256,256]{1,0:T(8,128)S(1)}, f32[256,256]{1,0:T(8,128)}, u32[]{:S(2)}) copy-start(f32[256,256]{1,0:T(8,128)} %param.16) | copy-start | bytes 786436
  7.2 618.9 %copy-start.3 = (f32[256,256]{1,0:T(8,128)S(1)}, f32[256,256]{1,0:T(8,128)}, u32[]{:S(2)}) copy-start(f32[256,256]{1,0:T(8,128)} %param.19) | copy-start | bytes 786436
  7.2 307.6 %all-gather.9.cloned.1.call-start = ((), (), s32[]{:S(2)}) async-start(), calls=%async_computation.5 | async-start | bytes 3170304 | tf_op jit(solution)/shard_map/all_gather | solution.py:30
  8.8 613.9 %all-gather.5.cloned.1.call-start = ((), (), s32[]{:S(2)}) async-start(), calls=%async_computation.3 | async-start | bytes 3170304 | tf_op jit(solution)/shard_map/all_gather | solution.py:25
  10.3 689.2 %all-gather.11.cloned.1.call-start = ((), (), s32[]{:S(2)}) async-start(), calls=%async_computation.6 | async-start | bytes 2162688 | tf_op jit(solution)/shard_map/all_gather | solution.py:46
  318.6 453.6 %all-gather.7.cloned.1.call-start = ((), (), s32[]{:S(2)}) async-start(), calls=%async_computation.4 | async-start | bytes 2162688 | tf_op jit(solution)/shard_map/all_gather | solution.py:45
  626.1 542.8 %reduce-scatter.6.cloned.1.call-start = ((), (), s32[]{:S(2)}) async-start(), calls=%async_computation.7 | async-start | bytes 4325376 | tf_op jit(solution)/shard_map/reduce_scatter | solution.py:58
  973.9 3.2 copy-start.1
  981.8 205.5 %reduce-scatter.8.cloned.1.call-start = ((), (), s32[]{:S(2)}) async-start(), calls=%async_computation.8 | async-start | bytes 1310720 | tf_op jit(solution)/shard_map/reduce_scatter | solution.py:57
  989.5 922.0 %reduce-scatter.10.cloned.1.call-start = ((), (), s32[]{:S(2)}) async-start(), calls=%async_computation.9 | async-start | bytes 6340608 | tf_op jit(solution)/shard_map/reduce_scatter | solution.py:65
  1181.2 6.1 copy-start.4
  1181.2 6.1 copy-start.5
  1181.2 730.3 %copy-start.6 = (f32[48,256]{1,0:T(8,128)S(1)}, f32[48,256]{1,0:T(8,128)}, u32[]{:S(2)}) copy-start(f32[48,256]{1,0:T(8,128)} %param.15) | copy-start | bytes 147460
  1181.2 730.3 %copy-start.7 = (f32[48,256]{1,0:T(8,128)S(1)}, f32[48,256]{1,0:T(8,128)}, u32[]{:S(2)}) copy-start(f32[48,256]{1,0:T(8,128)} %param.12) | copy-start | bytes 147460
  1181.2 730.3 %copy-start.8 = (f32[48,256]{1,0:T(8,128)S(1)}, f32[48,256]{1,0:T(8,128)}, u32[]{:S(2)}) copy-start(f32[48,256]{1,0:T(8,128)} %param.13) | copy-start | bytes 147460
  1181.2 730.3 %copy-start.9 = (f32[48,256]{1,0:T(8,128)S(1)}, f32[48,256]{1,0:T(8,128)}, u32[]{:S(2)}) copy-start(f32[48,256]{1,0:T(8,128)} %param.14) | copy-start | bytes 147460
Sparse Core Ops, SparseCore 0:
  10.3 304.4 all-gather.8
  317.1 305.5 all-gather.4
  626.4 73.0 all-gather.10
  703.0 69.1 all-gather.6
  981.9 186.9 reduce-scatter.5
  1171.1 16.0 reduce-scatter.7
  1189.7 721.7 reduce-scatter.9
where the time goes:
time: 1920 us
  waiting for transfers between devices  1640 us (85%)
  blocking collectives  196 us (10%)
  matrix products  39.6 us (2%)
  other arithmetic  21.6 us (1%)
    reduce_scatter x1, waiting for transfers between devices, per_device(): lax.psum_scatter(lax.dot_general(feat_s, dy, (((0,), (0,)), ((), ())), pr...  722 us
    all_gather x1, waiting for transfers between devices, per_device(): lax.all_gather(bot_t.astype(jnp.bfloat16), ('dp', 'fsdp'), axis=0, tiled=...  304 us
    all_gather x1, waiting for transfers between devices, per_device(): lax.all_gather(bot_s.astype(jnp.bfloat16), ('dp', 'fsdp'), axis=0, tiled=...  304 us
    psum x1, blocking collectives, per_device(): lax.psum((jnp.sum(expo_s, axis=1), jnp.sum(expo_t, axis=1)), 'fsdp')  181 us
    reduce_scatter x1, waiting for transfers between devices, per_device(): lax.psum_scatter(lax.dot_general(dz, cols_s, (((1,), (1,)), ((), ())), pr...  179 us
    all_gather x1, waiting for transfers between devices, per_device(): lax.all_gather(codes_s, 'fsdp', axis=0, tiled=True)  64 us
    all_gather x1, waiting for transfers between devices, per_device(): lax.all_gather(codes_t, 'fsdp', axis=0, tiled=True)  58.3 us
  transfers between devices with their start and end apart: 7, of which 7 were waited for; matrix products, arithmetic and copies ran while one was open for 2% of the time, Pallas kernels for 0%

commit v1 on v0

--- a/solution.py
+++ b/solution.py
@@ -27,7 +27,15 @@
     )
     yt = jnp.dot(
         cols_t,
-        lax.all_gather(bot_t.astype(jnp.bfloat16), ("dp", "fsdp"), axis=0, tiled=True),
+        jnp.concatenate(
+            lax.all_to_all(
+                jnp.stack([bot_t.astype(jnp.bfloat16)] * lax.axis_size(("dp", "fsdp"))),
+                ("dp", "fsdp"),
+                0,
+                0,
+            ),
+            axis=0,
+        ),
         preferred_element_type=jnp.float32,
     )
     norm_s = jnp.sqrt(jnp.sum(ys * ys, axis=1, keepdims=True) + 1e-06)

time: 1920 us -> 1620 us (0.84)
  waiting for transfers between devices: 1640 us -> 1290 us
  blocking collectives: 196 us -> 247 us
    all_gather x1 -> x0, waiting for transfers between devices: 304 us -> none  [per_device(): lax.all_gather(bot_t.astype(jnp.bfloat16), ('dp', 'fsdp'), axis=0, tiled=...]
    all_to_all x0 -> x1, blocking collectives: none -> 50.3 us  [per_device(): lax.all_to_all(jnp.stack([bot_t.astype(jnp.bfloat16)] * lax.axis_size(('d...]
    all_gather x1, waiting for transfers between devices: 304 us -> 264 us  [per_device(): lax.all_gather(bot_s.astype(jnp.bfloat16), ('dp', 'fsdp'), axis=0, tiled=...]
  transfers between devices with their start and end apart: 7 -> 6, of which waited for: 7 -> 6; matrix products, arithmetic and copies ran while one was open for 2% -> 2% of each run, Pallas kernels for 0% -> 0%
where the time goes in v1:
time: 1620 us
  waiting for transfers between devices  1290 us (80%)
  blocking collectives  247 us (15%)
  matrix products  37.3 us (2%)
  other arithmetic  21.9 us (1%)
    reduce_scatter x1, waiting for transfers between devices, per_device(): lax.psum_scatter(lax.dot_general(feat_s, dy, (((0,), (0,)), ((), ())), pr...  723 us
    all_gather x1, waiting for transfers between devices, per_device(): lax.all_gather(bot_s.astype(jnp.bfloat16), ('dp', 'fsdp'), axis=0, tiled=...  264 us
    psum x1, blocking collectives, per_device(): lax.psum((jnp.sum(expo_s, axis=1), jnp.sum(expo_t, axis=1)), 'fsdp')  181 us
    reduce_scatter x1, waiting for transfers between devices, per_device(): lax.psum_scatter(lax.dot_general(dz, cols_s, (((1,), (1,)), ((), ())), pr...  179 us
    all_gather x1, waiting for transfers between devices, per_device(): lax.all_gather(codes_s, 'fsdp', axis=0, tiled=True)  64.2 us
    all_gather x1, waiting for transfers between devices, per_device(): lax.all_gather(codes_t, 'fsdp', axis=0, tiled=True)  54.3 us
    all_to_all x1, blocking collectives, per_device(): lax.all_to_all(jnp.stack([bot_t.astype(jnp.bfloat16)] * lax.axis_size(('d...  50.3 us
  transfers between devices with their start and end apart: 6, of which 6 were waited for; matrix products, arithmetic and copies ran while one was open for 2% of the time, Pallas kernels for 0%

profile of v1, /device:TPU:96, one launch (start us, length us, event | category | flops | bytes accessed | tf_op | source)
XLA Modules:
  0.0 1621.4 jit_solution(5719281968295445555)
XLA Ops:
  7.2 0.0 copy-start
  7.2 0.0 copy-start.2
  7.2 0.0 all-gather.4.cloned.1.call-start
  7.2 1.6 convert_element_type.24
  8.8 0.0 all-gather.4.cloned.1.call-update
  8.8 0.0 all-gather.8.cloned.1.call-start
  8.9 0.8 convert_element_type.27
  9.7 0.2 stack.2
  9.9 50.3 %all_to_all.5 = bf16[128,48,256]{2,1,0:T(8,128)(2,1)S(1)} all-to-all(bf16[128,48,256]{2,1,0:T(8,128)(2,1)S(1)} %stack.2), channel_id=1, replica_groups=mesh['dp'=4,'fsdp'=32] {'dp','fsdp'}, dimensions={0} | all-to-all | bytes 6291456 | tf_op jit(solution)/shard_map/all_to_all | solution.py:31
  60.1 0.0 copy-start.3
  60.2 0.0 copy-done.2
  60.2 0.7 multiply_reduce_fusion.1
  60.8 0.7 divide_convert_fusion.1
  61.6 0.0 all-gather.8.cloned.1.call-update
  61.6 0.0 all-gather.6.cloned.1.call-start
  61.6 264.0 %all-gather.4.cloned.1.call-done = bf16[6144,256]{1,0:T(8,128)(2,1)} async-done(((bf16[48,256]{1,0:T(8,128)(2,1)}), bf16[6144,256]{1,0:T(8,128)(2,1)}) %all-gather.4.cloned.1.call-update) | async-done | bytes 3145744 | tf_op jit(solution)/shard_map/all_gather | solution.py:25
  325.6 0.0 copy-done
  325.6 2.5 multiply_reduce_fusion.2
  328.2 0.7 fusion.6
  328.9 0.0 all-gather.6.cloned.1.call-update
  328.9 0.0 reduce-scatter.6.cloned.1.call-start
  329.0 0.0 copy-done.3
  329.0 1.0 convert_element_type.29
  330.0 8.0 all_gather.17
  338.0 7.7 all_gather.19
  345.7 54.3 %all-gather.8.cloned.1.call-done = bf16[4096,256]{1,0:T(8,128)(2,1)} async-done(((bf16[128,256]{1,0:T(8,128)(2,1)}), bf16[4096,256]{1,0:T(8,128)(2,1)}) %all-gather.8.cloned.1.call-update) | async-done | bytes 2097168 | tf_op jit(solution)/shard_map/all_gather | solution.py:54
  400.0 8.7 fusion.1
  408.7 64.2 %all-gather.6.cloned.1.call-done = bf16[4096,256]{1,0:T(8,128)(2,1)} async-done(((bf16[128,256]{1,0:T(8,128)(2,1)}), bf16[4096,256]{1,0:T(8,128)(2,1)}) %all-gather.6.cloned.1.call-update) | async-done | bytes 2097168 | tf_op jit(solution)/shard_map/all_gather | solution.py:53
  472.9 8.7 fusion
  481.5 180.6 %all-reduce = (f32[4096]{0:T(1024)S(1)}, f32[4096]{0:T(1024)S(1)}) all-reduce(f32[4096]{0:T(1024)S(1)} %get-tuple-element.38, f32[4096]{0:T(1024)S(1)} %get-tuple-element.40), channel_id=1, replica_groups=mesh['dp'=4,'fsdp'=32] {'fsdp'}, use_global_device_ids=true, to_apply=%region_5.0 | all-reduce | flops 8192 | bytes 65536 | tf_op jit(solution)/shard_map/psum | solution.py:58
  662.1 12.5 multiply_convert_fusion
  674.6 0.0 copy-start.1
  674.6 3.2 copy-done.1
  677.8 4.6 fusion.9
  682.4 0.0 reduce-scatter.6.cloned.1.call-update
  682.5 0.2 reduce-scatter.8.cloned.1.call-start
  682.7 7.4 fusion.10
  690.1 0.0 reduce-scatter.8.cloned.1.call-update
  690.2 0.0 reduce-scatter.10.cloned.1.call-start
  690.2 179.4 %reduce-scatter.6.cloned.1.call-done = f32[128,256]{1,0:T(8,128)} async-done(((f32[4096,256]{1,0:T(8,128)}), f32[128,256]{1,0:T(8,128)}) %reduce-scatter.6.cloned.1.call-update) | async-done | bytes 131088 | tf_op jit(solution)/shard_map/reduce_scatter | solution.py:66
  869.7 1.1 multiply_reduce_fusion
  870.7 4.6 convolution_bitcast_fusion
  875.4 6.6 copy.39
  882.0 0.0 copy-start.4
  882.0 0.0 copy-start.5
  882.0 0.0 copy-start.6
  882.0 0.0 copy-start.7
  882.0 0.0 copy-start.8
  882.0 0.0 copy-start.9
  882.0 0.0 copy-start.10
  882.0 0.0 reduce-scatter.10.cloned.1.call-update
  882.0 5.8 reduce-scatter.8.cloned.1.call-done
  887.8 0.0 copy-done.4
  887.9 0.0 copy-done.5
  887.9 0.0 copy-done.6
  887.9 2.1 multiply_add_fusion
  889.9 723.1 %reduce-scatter.10.cloned.1.call-done = f32[48,256]{1,0:T(8,128)} async-done(((f32[6144,256]{1,0:T(8,128)}), f32[48,256]{1,0:T(8,128)}) %reduce-scatter.10.cloned.1.call-update) | async-done | bytes 49168 | tf_op jit(solution)/shard_map/reduce_scatter | solution.py:73
  1613.0 0.0 copy-done.7
  1613.0 0.0 copy-done.8
  1613.0 0.0 copy-done.9
  1613.0 0.0 copy-done.10
  1613.0 1.5 multiply_add_fusion.2
  (3 shorter events, 0.0 us)
Async XLA Ops:
  7.2 318.4 %copy-start = (bf16[128,6144]{1,0:T(8,128)(2,1)S(1)}, bf16[128,6144]{1,0:T(8,128)(2,1)}, u32[]{:S(2)}) copy-start(bf16[128,6144]{1,0:T(8,128)(2,1)} %param.10) | copy-start | bytes 4718596
  7.2 53.0 %copy-start.2 = (bf16[128,6144]{1,0:T(8,128)(2,1)S(1)}, bf16[128,6144]{1,0:T(8,128)(2,1)}, u32[]{:S(2)}) copy-start(bf16[128,6144]{1,0:T(8,128)(2,1)} %param.11) | copy-start | bytes 4718596
  7.2 318.4 %all-gather.4.cloned.1.call-start = ((), (), s32[]{:S(2)}) async-start(), calls=%async_computation.4 | async-start | bytes 3170304 | tf_op jit(solution)/shard_map/all_gather | solution.py:25
  8.8 391.2 %all-gather.8.cloned.1.call-start = ((), (), s32[]{:S(2)}) async-start(), calls=%async_computation.6 | async-start | bytes 2162688 | tf_op jit(solution)/shard_map/all_gather | solution.py:54
  60.1 268.8 %copy-start.3 = (f32[256,256]{1,0:T(8,128)S(1)}, f32[256,256]{1,0:T(8,128)}, u32[]{:S(2)}) copy-start(f32[256,256]{1,0:T(8,128)} %param.16) | copy-start | bytes 786436
  61.6 411.3 %all-gather.6.cloned.1.call-start = ((), (), s32[]{:S(2)}) async-start(), calls=%async_computation.5 | async-start | bytes 2162688 | tf_op jit(solution)/shard_map/all_gather | solution.py:53
  328.9 540.7 %reduce-scatter.6.cloned.1.call-start = ((), (), s32[]{:S(2)}) async-start(), calls=%async_computation.7 | async-start | bytes 4325376 | tf_op jit(solution)/shard_map/reduce_scatter | solution.py:66
  674.6 3.2 copy-start.1
  682.5 205.4 %reduce-scatter.8.cloned.1.call-start = ((), (), s32[]{:S(2)}) async-start(), calls=%async_computation.8 | async-start | bytes 1310720 | tf_op jit(solution)/shard_map/reduce_scatter | solution.py:65
  690.2 922.8 %reduce-scatter.10.cloned.1.call-start = ((), (), s32[]{:S(2)}) async-start(), calls=%async_computation.9 | async-start | bytes 6340608 | tf_op jit(solution)/shard_map/reduce_scatter | solution.py:73
  882.0 5.9 copy-start.4
  882.0 5.9 copy-start.5
  882.0 5.9 copy-start.6
  882.0 731.0 %copy-start.7 = (f32[48,256]{1,0:T(8,128)S(1)}, f32[48,256]{1,0:T(8,128)}, u32[]{:S(2)}) copy-start(f32[48,256]{1,0:T(8,128)} %param.15) | copy-start | bytes 147460
  882.0 731.0 %copy-start.8 = (f32[48,256]{1,0:T(8,128)S(1)}, f32[48,256]{1,0:T(8,128)}, u32[]{:S(2)}) copy-start(f32[48,256]{1,0:T(8,128)} %param.12) | copy-start | bytes 147460
  882.0 731.0 %copy-start.9 = (f32[48,256]{1,0:T(8,128)S(1)}, f32[48,256]{1,0:T(8,128)}, u32[]{:S(2)}) copy-start(f32[48,256]{1,0:T(8,128)} %param.13) | copy-start | bytes 147460
  882.0 731.0 %copy-start.10 = (f32[48,256]{1,0:T(8,128)S(1)}, f32[48,256]{1,0:T(8,128)}, u32[]{:S(2)}) copy-start(f32[48,256]{1,0:T(8,128)} %param.14) | copy-start | bytes 147460
Sparse Core Ops, SparseCore 0:
  10.3 315.2 all-gather.3
  329.3 70.7 all-gather.7
  403.7 69.1 all-gather.5
  682.6 187.0 reduce-scatter.5
  871.9 15.9 reduce-scatter.7
  890.2 722.7 reduce-scatter.9
